TPU v7x, 512 devices: a whole 4x4x16 slice. The times are simulated.
512 devices in a mesh: section: 16 (over z), tensor: 16 (over x, y_hi, core), dp: 2 (over y_lo).
Axes of the slice: x: 4, y: 4 (y_hi: 2, y_lo: 2; y = y_hi * 2 + y_lo), z: 16, core: 2. Of those that a mesh axis runs over, the one named last changes fastest.
Arguments:
- enc_out: float32 [2, 384, 4096], P('dp', 'tensor'), may hold values from -6 to 6
- gain: float32 [4096], replicated, may hold values from 0.5 to 1.5
- weights: bfloat16 [16, 4096, 4096], P('section', None, 'tensor'), may hold values from -0.09375 to 0.09375
- kv_grad: bfloat16 [16, 2, 384, 4096], P('section', 'dp', None, 'tensor'), may hold values from -4 to 4
Outputs:
- weight_grad: bfloat16 [16, 4096, 4096], P('section', None, 'tensor')
- enc_grad: bfloat16 [2, 384, 4096], P('dp', 'tensor', 'section')
All inputs are finite; a program needn't handle non-finite values.
Results may differ from a plain program's by a relative error of at most 0.025.
Values may be sent and summed in bfloat16 or wider, within the bound.
A program may use at most 64 MiB of HBM per device.

v0:
```python
import jax
import jax.numpy as jnp
from jax import lax
from jax.sharding import PartitionSpec as P


def per_device(enc_out, gain, weights, kv_grad):
    sections = lax.axis_size("section")
    section_id = lax.axis_index("section")
    active = (section_id >= sections // 4).astype(jnp.float32)
    enc_rows = enc_out[0]
    width = enc_rows.shape[1]
    inv_rms = lax.rsqrt(jnp.mean(enc_rows * enc_rows, axis=1, keepdims=True) + 1e-06)
    normed = enc_rows * inv_rms
    memory = (normed * gain).astype(jnp.bfloat16)
    kv_flat = kv_grad[0, 0]
    w_flat = weights[0]
    block = kv_flat
    local_sum = lax.dot_general(
        lax.all_gather(memory, "tensor", axis=0, tiled=True),
        block,
        (((0,), (0,)), ((), ())),
        preferred_element_type=jnp.float32,
    )
    total = lax.psum((local_sum * active).astype(jnp.bfloat16), "dp")
    weight_grad = total.reshape(weights.shape)
    block = kv_flat
    partial_sum = lax.psum_scatter(
        (
            lax.dot_general(
                block, w_flat, (((1,), (1,)), ((), ())), preferred_element_type=jnp.float32
            )
            * active
        ).astype(jnp.bfloat16),
        "tensor",
        scatter_dimension=0,
        tiled=True,
    )
    col_count = width // sections
    col_start = section_id * col_count
    normed_cols = lax.dynamic_slice_in_dim(normed, col_start, col_count, 1)
    gain_cols = lax.dynamic_slice_in_dim(gain, col_start, col_count, 0)
    own_cols = lax.psum_scatter(partial_sum, "section", scatter_dimension=1, tiled=True).astype(
        jnp.float32
    )
    local_dot = jnp.sum(normed_cols * gain_cols * own_cols, axis=1, keepdims=True)
    row_dot = lax.psum(local_dot, "section")
    scaled = gain_cols * own_cols
    result = inv_rms * (scaled - normed_cols * (row_dot / width))
    return (weight_grad, result.astype(jnp.bfloat16)[None])


def solution(mesh):
    return jax.shard_map(
        per_device,
        mesh=mesh,
        in_specs=(
            P("dp", "tensor", None),
            P(),
            P("section", None, "tensor"),
            P("section", "dp", None, "tensor"),
        ),
        out_specs=(P("section", None, "tensor"), P("dp", "tensor", "section")),
        check_vma=False,
    )
```

profile of v0, /device:TPU:1, one launch (start us, length us, event | category | flops | bytes accessed | tf_op | source)
XLA Modules:
  0.0 353.5 jit_solution(4860401714487688542)
XLA Ops:
  7.2 0.0 copy-start
  7.2 0.0 reduce-scatter.3.cloned.1.call-start
  7.2 1.5 copy-done
  8.8 3.6 %multiply_convert_fusion = bf16[384,4096]{1,0:T(8,128)(2,1)} fusion(f32[]{:T(128)S(6)} %convert_element_type.19, bf16[1,4096,256]{2,1,0:T(8,128)(2,1)S(1)} %copy-done, bf16[1,1,384,256]{3,2,1,0:T(8,128)(2,1)} %param.7), kind=kOutput, calls=%fused_computation | convolution fusion | flops 808452096 | bytes 5439492 | tf_op jit(solution)/shard_map/dot_general | solution.py:30
  12.4 0.0 copy-start.1
  12.4 0.0 copy-start.3
  12.4 0.0 copy-start.2
  12.4 0.0 reduce-scatter.3.cloned.1.call-update
  12.4 0.0 all-gather.2.cloned.1.call-start
  12.5 0.9 copy-done.1
  13.4 0.1 fusion.3
  13.6 0.0 copy-done.3
  13.6 0.8 multiply_convert_fusion.1
  14.4 0.0 all-gather.2.cloned.1.call-update
  14.4 0.0 reduce-scatter.5.cloned.1.call-start
  14.4 101.1 %reduce-scatter.3.cloned.1.call-done = bf16[24,4096]{1,0:T(8,128)(2,1)} async-done(((bf16[384,4096]{1,0:T(8,128)(2,1)}), bf16[24,4096]{1,0:T(8,128)(2,1)}) %reduce-scatter.3.cloned.1.call-update) | async-done | bytes 196624 | tf_op jit(solution)/shard_map/reduce_scatter | solution.py:28
  115.5 0.0 reduce-scatter.5.cloned.1.call-update
  115.5 0.0 all-reduce.2.cloned.1.call-start
  115.6 72.0 %all-gather.2.cloned.1.call-done = bf16[384,4096]{1,0:T(8,128)(2,1)} async-done(((bf16[24,4096]{1,0:T(8,128)(2,1)}), bf16[384,4096]{1,0:T(8,128)(2,1)}) %all-gather.2.cloned.1.call-update) | async-done | bytes 3145744 | tf_op jit(solution)/shard_map/all_gather | solution.py:20
  187.6 0.0 copy-done.2
  187.6 4.5 %fusion.1 = bf16[1,4096,256]{2,1,0:T(8,128)(2,1)} fusion(bf16[384,4096]{1,0:T(8,128)(2,1)} %all-gather.2.cloned.1.call-done, f32[]{:T(128)S(6)} %convert_element_type.19, bf16[1,1,384,256]{3,2,1,0:T(8,128)(2,1)S(1)} %copy-done.2), kind=kOutput, calls=%fused_computation.3 | convolution fusion | flops 807403520 | bytes 5439492 | tf_op jit(solution)/shard_map/dot_general | solution.py:19
  192.1 0.0 all-reduce.2.cloned.1.call-update
  192.1 0.1 dynamic_slice.6
  192.2 54.2 %reduce-scatter.5.cloned.1.call-done = bf16[24,256]{1,0:T(8,128)(2,1)} async-done(((bf16[24,4096]{1,0:T(8,128)(2,1)}), bf16[24,256]{1,0:T(8,128)(2,1)}) %reduce-scatter.5.cloned.1.call-update) | async-done | bytes 12304 | tf_op jit(solution)/shard_map/reduce_scatter | solution.py:43
  246.3 0.8 fusion.9
  247.2 21.4 %psum.15 = f32[24,1]{0,1:T(1,128)S(1)} all-reduce(f32[24,1]{0,1:T(1,128)S(1)} %bitcast.22), channel_id=1, replica_groups=mesh['section'=16,'tensor'=16,'dp'=2] {'section'}, use_global_device_ids=true, to_apply=%region_5.0 | all-reduce | flops 24 | bytes 192 | tf_op jit(solution)/shard_map/psum | solution.py:47
  268.6 1.4 fusion.10
  270.0 74.0 %all-reduce.2.cloned.1.call-done = bf16[1,4096,256]{2,1,0:T(8,128)(2,1)} async-done(((bf16[1,4096,256]{2,1,0:T(8,128)(2,1)}), bf16[1,4096,256]{2,1,0:T(8,128)(2,1)}) %all-reduce.2.cloned.1.call-update) | async-done | bytes 2097168 | tf_op jit(solution)/shard_map/psum | solution.py:25
  343.9 3.0 copy.7
  (2 shorter events, 0.0 us)
Async XLA Ops:
  7.2 1.6 copy-start
  7.2 108.3 %reduce-scatter.3.cloned.1.call-start = ((), (), s32[]{:S(2)}) async-start(), calls=%async_computation.4 | async-start | bytes 3342336 | tf_op jit(solution)/shard_map/reduce_scatter | solution.py:28
  12.4 1.0 copy-start.1
  12.4 1.2 copy-start.3
  12.4 175.1 %copy-start.2 = (bf16[1,1,384,256]{3,2,1,0:T(8,128)(2,1)S(1)}, bf16[1,1,384,256]{3,2,1,0:T(8,128)(2,1)}, u32[]{:S(2)}) copy-start(bf16[1,1,384,256]{3,2,1,0:T(8,128)(2,1)} %param.7) | copy-start | bytes 589828
  12.4 175.1 %all-gather.2.cloned.1.call-start = ((), (), s32[]{:S(2)}) async-start(), calls=%async_computation.2 | async-start | bytes 3342336 | tf_op jit(solution)/shard_map/all_gather | solution.py:20
  14.4 232.0 %reduce-scatter.5.cloned.1.call-start = ((), (), s32[]{:S(2)}) async-start(), calls=%async_computation.5 | async-start | bytes 208896 | tf_op jit(solution)/shard_map/reduce_scatter | solution.py:43
  115.5 228.4 %all-reduce.2.cloned.1.call-start = ((), (), s32[]{:S(2)}) async-start(), calls=%async_computation.3 | async-start | bytes 4194304 | tf_op jit(solution)/shard_map/psum | solution.py:25
Sparse Core Ops, SparseCore 0:
  12.9 102.5 reduce-scatter.2
  119.4 68.1 all-gather.1
  190.3 55.9 reduce-scatter.4
  249.9 93.9 all-reduce.1
where the time goes:
time: 354 us
  waiting for transfers between devices  301 us (85%)
  blocking collectives  21.4 us (6%)
  between operations  13.8 us (4%)
  matrix products  8.16 us (2%)
  local copies, waits for them, and re-layouts  5.58 us (2%)
    reduce_scatter x1, waiting for transfers between devices, per_device(): lax.psum_scatter((lax.dot_general(block, w_flat, (((1,), (1,)), ((), ()))...  101 us
    psum x1, waiting for transfers between devices, per_device(): total = lax.psum((local_sum * active).astype(jnp.bfloat16), 'dp')  74 us
    all_gather x1, waiting for transfers between devices, per_device(): lax.all_gather(memory, 'tensor', axis=0, tiled=True)  72 us
    reduce_scatter x1, waiting for transfers between devices, per_device(): lax.psum_scatter(partial_sum, 'section', scatter_dimension=1, tiled=True)  54.2 us
    psum x1, blocking collectives, per_device(): row_dot = lax.psum(local_dot, 'section')  21.4 us
  transfers between devices with their start and end apart: 4, of which 4 were waited for; matrix products, arithmetic and copies ran while one was open for 2% of the time, Pallas kernels for 0%

commit v1 on v0

v1 whole, which is shorter than its diff:
```python
import functools

import jax
import jax.numpy as jnp
from jax import lax
from jax.experimental import pallas as pl
from jax.experimental.pallas import tpu as pltpu
from jax.sharding import PartitionSpec as P

F32, BF16 = jnp.float32, jnp.bfloat16
X, Y = 4, 4
NT = (((1,), (1,)), ((), ()))
TN = (((0,), (0,)), ((), ()))


def kernel(
    nz,
    enc_ref,
    gain_ref,
    w_ref,
    kv_ref,
    wg_ref,
    eg_ref,
    xs,
    xr,
    mem,
    kvs,
    ws,
    first,
    run,
    gs,
    gr,
    hs,
    hr,
    ow,
    loc_sem,
    x_sem,
    kv_sem,
    w_ss,
    w_rs,
    ag_ss,
    ag_rs,
    z_ss,
    z_rs,
    t_ss,
    t_rs,
    h_ss,
    h_rs,
    o_sem,
):
    z, t, b = lax.axis_index("section"), lax.axis_index("tensor"), lax.axis_index("dp")
    x, yh, c = t // 4, (t // 2) % 2, t % 2
    y = yh * 2 + b
    o = 1 - c
    nt = X * 4
    rows, width = enc_ref.shape
    half = nz // 2
    cols = half * 128
    tok = kvs.shape[2]
    sub = tok // 2
    act = (z >= nz // 4).astype(F32)

    def dev(x_, y_, z_, c_):
        return (z_, x_ * 4 + (y_ // 2) * 2 + c_, y_ % 2)

    def remote(src, dst, ss, rs, to):
        return pltpu.make_async_remote_copy(
            src_ref=src,
            dst_ref=dst,
            send_sem=ss,
            recv_sem=rs,
            device_id=to,
            device_id_type=pl.DeviceIdType.MESH,
        )

    me = dev(x, y, z, c)
    other = dev(x, y, z, o)
    sent = []

    def send(src, dst, ss, rs, to):
        copy = remote(src, dst, ss, rs, to)
        copy.start()
        sent.append(copy)

    def arrived(dst, ss, rs):
        remote(dst, dst, ss, rs, other).wait_recv()

    kv_load = pltpu.make_async_copy(kv_ref, kvs.at[c, b], loc_sem.at[0])
    kv_load.start()
    w_load = pltpu.make_async_copy(w_ref.at[:, c], ws.at[c], loc_sem.at[1])
    w_load.start()

    barrier = pltpu.get_barrier_semaphore()

    def greet(to):
        pl.semaphore_signal(barrier, inc=1, device_id=to, device_id_type=pl.DeviceIdType.MESH)

    for i in range(1, nt):
        greet((z, lax.rem(t + i, nt), b))
    for i in range(1, nz):
        greet((lax.rem(z + i, nz), t, b))
    greet(dev(x, (y + 1) % Y, z, c))
    greet(dev(x, (y + 3) % Y, z, c))

    enc = enc_ref[...]
    inv = lax.rsqrt(jnp.mean(enc * enc, axis=1, keepdims=True) + 1e-06)
    own_cols = []
    for s in range(nz):
        part = (enc[:, s * 256 : (s + 1) * 256] * inv) * gain_ref[:, s * 256 : (s + 1) * 256]
        lo, hi = part[:, :128], part[:, 128:]
        own_cols.append(jnp.where(c == 0, lo, hi))
        xs[:, s * 128 : (s + 1) * 128] = jnp.where(c == 0, hi, lo).astype(BF16)

    pl.semaphore_wait(barrier, nt - 1 + nz - 1 + 2)

    send(xs, xr, x_sem.at[0], x_sem.at[1], other)
    kv_load.wait()
    send(kvs.at[c, b], kvs.at[c, b], kv_sem.at[0], kv_sem.at[1], other)
    order = [half]
    for m in range(half - 1, 0, -1):
        order += [m, nz - m]
    order += [0]
    for m in order:
        d = lax.rem(z + m, nz)
        send(w_ref.at[d, o], ws.at[c, d], w_ss.at[d], w_rs.at[d], other)
    dp_peer = dev(x, yh * 2 + (1 - b), z, c)

    def at_xy(h, f, g):
        return (f, g) if h == 0 else (g, f)

    def slot(h, f, g):
        x_, y_ = at_xy(h, f, g)
        return mem.at[h, y_ % 2, x_, y_ // 2]

    def place(h, f, g):
        x_, y_ = at_xy(h, f, g)
        return dev(x_, y_, z, c)

    fg = [(x, y), (y, x)]
    half_cols = (pl.ds(0, cols // 2), pl.ds(cols // 2, cols // 2))

    def sems(h, k):
        return ag_ss.at[h, k], ag_rs.at[h, k]

    STEP = (1, 3)

    def second(h, i):
        f, g = fg[h]
        f_ = (f + (0, 3, 1, 2)[i]) % 4
        for d in range(2):
            s = slot(h, f_, g)
            send(s, s, *sems(h, 4 + 2 * i + d), place(h, f, (g + STEP[d]) % 4))

    def gather0(h):
        f, g = fg[h]
        s = slot(h, f, g)
        for d in range(2):
            send(s, s, *sems(h, d), place(h, (f + STEP[d]) % 4, g))
        second(h, 0)

    def gather1(h):
        f, g = fg[h]
        for d in range(2):
            s = slot(h, (f + STEP[1 - d]) % 4, g)
            arrived(s, *sems(h, d))
            s = s.at[:, half_cols[d]]
            send(s, s, *sems(h, 2 + d), place(h, (f + STEP[d]) % 4, g))
        second(h, 1)
        second(h, 2)

    def gather2(h):
        f, g = fg[h]
        for d in range(2):
            arrived(slot(h, (f + 2) % 4, g).at[:, half_cols[d]], *sems(h, 2 + d))
        second(h, 3)

    def gather3(h, i):
        f, g = fg[h]
        f_ = (f + (0, 3, 1, 2)[i]) % 4
        for d in range(2):
            s = slot(h, f_, (g + STEP[1 - d]) % 4)
            arrived(s, *sems(h, 4 + 2 * i + d))
            s = s.at[:, half_cols[d]]
            send(s, s, *sems(h, 12 + 2 * i + d), place(h, f, (g + STEP[d]) % 4))

    def gather4(h):
        f, g = fg[h]
        for i in range(4):
            f_ = (f + (0, 3, 1, 2)[i]) % 4
            for d in range(2):
                s = slot(h, f_, (g + 2) % 4).at[:, half_cols[d]]
                arrived(s, *sems(h, 12 + 2 * i + d))

    arrived(xr, x_sem.at[0], x_sem.at[1])
    for h in range(2):
        for s in range(half):
            mine = own_cols[h * half + s]
            theirs = xr[:, (h * half + s) * 128 : (h * half + s + 1) * 128].astype(F32)
            both = jnp.concatenate(
                [jnp.where(c == 0, mine, theirs), jnp.where(c == 0, theirs, mine)], axis=0
            )
            mem[h, b, x, yh, :, s * 128 : (s + 1) * 128] = both.astype(BF16)
        gather0(h)
    send(kvs.at[c, b], kvs.at[c, b], kv_sem.at[2], kv_sem.at[3], dp_peer)

    w_load.wait()
    arrived(kvs.at[o, b], kv_sem.at[0], kv_sem.at[1])

    def term(d):
        arrived(ws.at[o, d], w_ss.at[d], w_rs.at[d])
        out = lax.dot_general(kvs[0, b], ws[0, d], NT, preferred_element_type=F32)
        out += lax.dot_general(kvs[1, b], ws[1, d], NT, preferred_element_type=F32)
        return out * act

    def z_step(m):
        to_up = term(lax.rem(z + m, nz))
        to_down = to_up if 2 * m == nz else term(lax.rem(z + nz - m, nz))
        for j in range(2):
            for d in range(2):
                if m == half and d != j:
                    continue
                mine = (to_up, to_down)[d][j * sub : (j + 1) * sub]
                if m == half or (m == half - 1 and d != j):
                    src = first.at[d, j]
                    src[...] = mine.astype(BF16)
                else:
                    src = run.at[d, j, m]
                    arrived(src, z_ss.at[d, j, m], z_rs.at[d, j, m])
                    src[...] = (src[...].astype(F32) + mine).astype(BF16)
                to = dev(x, y, lax.rem(z + (1, nz - 1)[d], nz), c)
                send(src, run.at[d, j, m - 1], z_ss.at[d, j, m - 1], z_rs.at[d, j, m - 1], to)

    def kv_forward():
        got = kvs.at[c, 1 - b]
        arrived(got, kv_sem.at[2], kv_sem.at[3])
        send(got, got, kv_sem.at[4], kv_sem.at[5], other)

    def both(f, *args):
        for h in range(2):
            f(h, *args)

    events = {
        half - 1: [lambda: both(gather1)],
        half - 2: [lambda: both(gather2), lambda: both(gather3, 0), kv_forward],
        half - 4: [lambda: both(gather3, 1), lambda: both(gather3, 2)],
        half - 5: [lambda: both(gather3, 3)],
    }
    for m in range(half, 0, -1):
        z_step(m)
        for event in events.get(m, ()):
            event()

    last = term(z)
    for j in range(2):
        total = last[j * sub : (j + 1) * sub]
        for d in range(2):
            arrived(run.at[d, j, 0], z_ss.at[d, j, 0], z_rs.at[d, j, 0])
            total += run[d, j, 0].astype(F32)
        for i in range(nt // 2):
            gs[j * (nt // 2) + i] = total[i * rows : (i + 1) * rows].astype(BF16)
    for i in range(1, nt):
        to = lax.rem(t + i, nt)
        send(gs.at[to], gr.at[t], t_ss.at[to], t_rs.at[t], (z, to, b))
    gr[t] = gs[t]

    outs = []

    def weight_part(h):
        both_mem = mem.at[h]
        for k in range(cols // 256):
            lhs = both_mem[:, :, :, :, k * 256 : (k + 1) * 256].reshape(2 * tok, 256)
            for side in range(2):
                core = (c, o)[side]
                rhs = kvs[core].reshape(2 * tok, 256)
                out = lax.dot_general(lhs, rhs, TN, preferred_element_type=F32) * act
                ow[side, h * half + 2 * k] = out[:128].astype(BF16)
                ow[side, h * half + 2 * k + 1] = out[128:].astype(BF16)
        part = pl.ds(h * half, half)
        copy = pltpu.make_async_copy(ow.at[0, part], wg_ref.at[part, c], loc_sem.at[2 + h])
        copy.start()
        outs.append(copy)
        send(ow.at[1, part], wg_ref.at[part, c], o_sem.at[0, h], o_sem.at[1, h], other)

    gather4(0)
    arrived(kvs.at[o, 1 - b], kv_sem.at[4], kv_sem.at[5])
    weight_part(0)

    for i in range(1, nt):
        frm = lax.rem(t + i, nt)
        arrived(gr.at[frm], t_ss.at[frm], t_rs.at[frm])
    sums = [jnp.zeros((rows, 128), F32), jnp.zeros((rows, 128), F32)]
    for i in range(nt):
        sums[i % 2] += gr[i].astype(F32)
    own = jnp.concatenate(sums, axis=1)
    mine = pl.ds(pl.multiple_of(z * 256, 256), 256)
    normed = enc_ref[:, mine] * inv
    scaled = gain_ref[:, mine] * own
    dots = jnp.sum(normed * scaled, axis=1, keepdims=True)
    diagonal = lax.broadcasted_iota(jnp.int32, (rows, 128), 0) == lax.broadcasted_iota(
        jnp.int32, (rows, 128), 1
    )
    hs[...] = jnp.sum(jnp.where(diagonal, dots, 0.0), axis=0, keepdims=True)
    for i in range(1, nz):
        to = lax.rem(z + i, nz)
        send(hs, hr.at[z], h_ss.at[to], h_rs.at[z], (to, t, b))
    hr[z] = hs[...]

    gather4(1)
    weight_part(1)

    for i in range(1, nz):
        frm = lax.rem(z + i, nz)
        arrived(hr.at[frm], h_ss.at[frm], h_rs.at[frm])
    row = jnp.zeros((1, 128), F32)
    for i in range(nz):
        row += hr[i]
    row_dot = jnp.sum(jnp.where(diagonal, row, 0.0), axis=1, keepdims=True) * (1.0 / width)
    eg_ref[...] = (inv * (scaled - normed * row_dot)).astype(BF16)

    for h in range(2):
        part = pl.ds(h * half, half)
        arrived(wg_ref.at[part, o], o_sem.at[0, h], o_sem.at[1, h])
    for copy in outs:
        copy.wait()
    for copy in sent:
        copy.wait_send()


def solution(mesh):
    nz, nt = mesh.shape["section"], mesh.shape["tensor"]

    def per_device(enc_out, gain, weights, kv_grad):
        _, rows, width = enc_out.shape
        tok, hd = kv_grad.shape[2:]
        half = nz // 2
        dma = pltpu.SemaphoreType.DMA
        wg, eg = pl.pallas_call(
            functools.partial(kernel, nz),
            out_shape=(
                jax.ShapeDtypeStruct((nz, 2, 128, hd), BF16),
                jax.ShapeDtypeStruct((rows, 256), BF16),
            ),
            in_specs=[
                pl.BlockSpec(memory_space=pltpu.VMEM),
                pl.BlockSpec(memory_space=pltpu.VMEM),
                pl.BlockSpec(memory_space=pl.ANY),
                pl.BlockSpec(memory_space=pl.ANY),
            ],
            out_specs=(
                pl.BlockSpec(memory_space=pl.ANY),
                pl.BlockSpec(memory_space=pltpu.VMEM),
            ),
            scratch_shapes=[
                pltpu.VMEM((rows, width // 2), BF16),
                pltpu.VMEM((rows, width // 2), BF16),
                pltpu.VMEM((2, 2, X, 2, 2 * rows, half * 128), BF16),
                pltpu.VMEM((2, 2, tok, hd), BF16),
                pltpu.VMEM((2, nz, 128, hd), BF16),
                pltpu.VMEM((2, 2, tok // 2, 128), BF16),
                pltpu.VMEM((2, 2, half, tok // 2, 128), BF16),
                pltpu.VMEM((nt, rows, 128), BF16),
                pltpu.VMEM((nt, rows, 128), BF16),
                pltpu.VMEM((1, 128), F32),
                pltpu.VMEM((nz, 1, 128), F32),
                pltpu.VMEM((2, nz, 128, hd), BF16),
                dma((4,)),
                dma((2,)),
                dma((6,)),
                dma((nz,)),
                dma((nz,)),
                dma((2, 20)),
                dma((2, 20)),
                dma((2, 2, half)),
                dma((2, 2, half)),
                dma((nt,)),
                dma((nt,)),
                dma((nz,)),
                dma((nz,)),
                dma((2, 2)),
            ],
            compiler_params=pltpu.CompilerParams(
                collective_id=0, has_side_effects=True, vmem_limit_bytes=40 * 1024 * 1024
            ),
            cost_estimate=pl.CostEstimate(
                flops=6 * tok * width * hd, bytes_accessed=8 * width * hd, transcendentals=0
            ),
        )(
            enc_out[0],
            gain.reshape(1, width),
            weights.reshape(nz, 2, 128, hd),
            kv_grad[0, 0],
        )
        return wg.reshape(1, width, hd), eg[None]

    return jax.shard_map(
        per_device,
        mesh=mesh,
        in_specs=(
            P("dp", "tensor", None),
            P(),
            P("section", None, "tensor"),
            P("section", "dp", None, "tensor"),
        ),
        out_specs=(P("section", None, "tensor"), P("dp", "tensor", "section")),
        check_vma=False,
    )
```

time: 354 us -> 76.1 us (0.21)
  waiting for transfers between devices: 301 us -> 0 us
  Pallas kernels: 0 us -> 69.1 us
  blocking collectives: 21.4 us -> 0 us
  between operations: 13.8 us -> 0.65 us
  matrix products: 8.16 us -> 0 us
    reduce_scatter x2 -> x0, waiting for transfers between devices: 155 us -> none  [the longest x1 101 us: per_device(): lax.psum_scatter((lax.dot_general(block, w_flat, (((1,), (1,)), ((), ()))...]
    psum x1 -> x0, waiting for transfers between devices: 74 us -> none  [per_device(): total = lax.psum((local_sum * active).astype(jnp.bfloat16), 'dp')]
    all_gather x1 -> x0, waiting for transfers between devices: 72 us -> none  [per_device(): lax.all_gather(memory, 'tensor', axis=0, tiled=True)]
    pallas_call x0 -> x1, Pallas kernels: none -> 69.1 us  [per_device(): pl.pallas_call(functools.partial(kernel, nz), out_shape=(jax.ShapeDtypeSt...]
    psum x1 -> x0, blocking collectives: 21.4 us -> none  [per_device(): row_dot = lax.psum(local_dot, 'section')]
    dot_general x2 -> x0, matrix products: 8.16 us -> none  [the longest x1 4.51 us: per_device(): lax.dot_general(lax.all_gather(memory, 'tensor', axis=0, tiled=True), blo...]
  transfers between devices with their start and end apart: 4 -> 0, of which waited for: 4 -> 0; matrix products, arithmetic and copies ran while one was open for 2% -> 0% of each run, Pallas kernels for 0% -> 0%
where the time goes in v1:
time: 76.1 us; the launch traced here: 75.9 us
  Pallas kernels  69.1 us (91%)
  local copies, waits for them, and re-layouts  6.14 us (8%)
    pallas_call x1, Pallas kernels, per_device(): pl.pallas_call(functools.partial(kernel, nz), out_shape=(jax.ShapeDtypeSt...  69.1 us
    unnamed x10, local copies, waits for them, and re-layouts  6.14 us

profile of v1, /device:TPU:1, one launch (start us, length us, event | category | flops | bytes accessed | tf_op | source)
XLA Modules:
  0.0 75.9 jit_solution(11188259644314671730)
XLA Ops:
  0.6 0.0 copy-start
  0.6 1.6 %copy-done = bf16[1,4096,256]{2,1,0:T(8,128)(2,1)S(1)} copy-done((bf16[1,4096,256]{2,1,0:T(8,128)(2,1)S(1)}, bf16[1,4096,256]{2,1,0:T(8,128)(2,1)}, u32[]{:S(2)}) %copy-start) | copy-done | bytes 2097176
  2.2 0.0 copy-start.1
  2.2 1.0 %copy-done.1 = f32[1,24,4096]{2,1,0:T(8,128)S(1)} copy-done((f32[1,24,4096]{2,1,0:T(8,128)S(1)}, f32[1,24,4096]{2,1,0:T(8,128)}, u32[]{:S(2)}) %copy-start.1) | copy-done | bytes 393240
  3.2 0.0 copy-start.2
  3.2 0.9 %copy-done.2 = bf16[1,1,384,256]{3,2,1,0:T(8,128)(2,1)S(1)} copy-done((bf16[1,1,384,256]{3,2,1,0:T(8,128)(2,1)S(1)}, bf16[1,1,384,256]{3,2,1,0:T(8,128)(2,1)}, u32[]{:S(2)}) %copy-start.2) | copy-done | bytes 196632
  4.1 0.0 copy-start.3
  4.1 0.7 copy-done.3
  4.9 69.1 %shard_map.59 = (bf16[16,2,128,256]{3,2,1,0:T(8,128)(2,1)S(1)}, bf16[24,256]{1,0:T(8,128)(2,1)S(1)}) custom-call(f32[24,4096]{1,0:T(8,128)S(1)} %bitcast.9, f32[1,4096]{1,0:T(1,128)S(1)} %bitcast.11, bf16[16,2,128,256]{3,2,1,0:T(8,128)(2,1)S(1)} %bitcast.8, bf16[384,256]{1,0:T(8,128)(2,1)S(1)} %bitcast.10), custom_call_target="tpu_custom_call" | custom-call | flops 2415919104 | bytes 8388608 | tf_op jit(solution)/shard_map/pallas_call | solution.py:337
  74.0 1.3 %copy.8 = bf16[1,4096,256]{2,1,0:T(8,128)(2,1)} copy(bf16[1,4096,256]{2,1,0:T(8,128)(2,1)S(1)} %bitcast.6) | data formatting | bytes 4194304
  75.3 0.6 copy.9
Async XLA Ops:
  0.6 1.6 %copy-start = (bf16[1,4096,256]{2,1,0:T(8,128)(2,1)S(1)}, bf16[1,4096,256]{2,1,0:T(8,128)(2,1)}, u32[]{:S(2)}) copy-start(bf16[1,4096,256]{2,1,0:T(8,128)(2,1)} %param.6) | copy-start | bytes 6291460
  2.2 1.0 %copy-start.1 = (f32[1,24,4096]{2,1,0:T(8,128)S(1)}, f32[1,24,4096]{2,1,0:T(8,128)}, u32[]{:S(2)}) copy-start(f32[1,24,4096]{2,1,0:T(8,128)} %param.4) | copy-start | bytes 1179652
  3.2 0.9 %copy-start.2 = (bf16[1,1,384,256]{3,2,1,0:T(8,128)(2,1)S(1)}, bf16[1,1,384,256]{3,2,1,0:T(8,128)(2,1)}, u32[]{:S(2)}) copy-start(bf16[1,1,384,256]{3,2,1,0:T(8,128)(2,1)} %param.7) | copy-start | bytes 589828
  4.1 0.7 copy-start.3

commit v2 on v1

v2 whole, which is shorter than its diff:
```python
import functools

import jax
import jax.numpy as jnp
from jax import lax
from jax.experimental import pallas as pl
from jax.experimental.pallas import tpu as pltpu
from jax.sharding import PartitionSpec as P

F32, BF16 = jnp.float32, jnp.bfloat16
X, Y = 4, 4
NT = (((1,), (1,)), ((), ()))
TN = (((0,), (0,)), ((), ()))
PARTS = 4


def kernel(
    nz,
    enc_hbm,
    gain_hbm,
    w_ref,
    kv_ref,
    wg_ref,
    eg_ref,
    enc_ref,
    gain_ref,
    xs,
    xr,
    mem,
    kvs,
    ws,
    tm,
    first,
    run,
    gs,
    gr,
    qa,
    hs,
    hr,
    qs,
    qr,
    ow,
    loc_sem,
    x_sem,
    kv_sem,
    w_ss,
    w_rs,
    ag_ss,
    ag_rs,
    z_ss,
    z_rs,
    t_ss,
    t_rs,
    q_ss,
    q_rs,
    h_ss,
    h_rs,
    o_sem,
):
    z, t, b = lax.axis_index("section"), lax.axis_index("tensor"), lax.axis_index("dp")
    x, yh, c = t // 4, (t // 2) % 2, t % 2
    y = yh * 2 + b
    o = 1 - c
    nt = X * 4
    rows, width = enc_ref.shape
    half = nz // 2
    cols = half * 128
    tok = kvs.shape[2]
    sub = tok // PARTS
    act = (z >= nz // 4).astype(F32)

    def dev(x_, y_, z_, c_):
        return (z_, x_ * 4 + (y_ // 2) * 2 + c_, y_ % 2)

    def remote(src, dst, ss, rs, to):
        return pltpu.make_async_remote_copy(
            src_ref=src,
            dst_ref=dst,
            send_sem=ss,
            recv_sem=rs,
            device_id=to,
            device_id_type=pl.DeviceIdType.MESH,
        )

    other = dev(x, y, z, o)
    sent = []

    def send(src, dst, ss, rs, to):
        copy = remote(src, dst, ss, rs, to)
        copy.start()
        sent.append(copy)

    def arrived(dst, ss, rs):
        remote(dst, dst, ss, rs, other).wait_recv()

    barrier = pltpu.get_barrier_semaphore()

    def greet(to):
        pl.semaphore_signal(barrier, inc=1, device_id=to, device_id_type=pl.DeviceIdType.MESH)

    for i in (8, 7, 9, 6, 10, 5, 11, 4, 12, 3, 13, 2, 14, 1, 15):
        greet((lax.rem(z + i, nz), t, b))
    for i in range(1, nt):
        greet((z, lax.rem(t + i, nt), b))
    greet(dev(x, (y + 1) % Y, z, c))
    greet(dev(x, (y + 3) % Y, z, c))

    enc_load = pltpu.make_async_copy(enc_hbm, enc_ref, loc_sem.at[2])
    enc_load.start()
    gain_load = pltpu.make_async_copy(gain_hbm, gain_ref, loc_sem.at[3])
    gain_load.start()
    kv_load = pltpu.make_async_copy(kv_ref, kvs.at[c, b], loc_sem.at[0])
    kv_load.start()
    w_load = pltpu.make_async_copy(w_ref.at[:, c], ws.at[c], loc_sem.at[1])
    w_load.start()

    enc_load.wait()
    gain_load.wait()
    enc = enc_ref[...]
    inv = lax.rsqrt(jnp.mean(enc * enc, axis=1, keepdims=True) + 1e-06)
    own_cols = []
    for s in range(nz):
        part = (enc[:, s * 256 : (s + 1) * 256] * inv) * gain_ref[:, s * 256 : (s + 1) * 256]
        lo, hi = part[:, :128], part[:, 128:]
        own_cols.append(jnp.where(c == 0, lo, hi))
        xs[:, s * 128 : (s + 1) * 128] = jnp.where(c == 0, hi, lo).astype(BF16)
    kv_load.wait()

    pl.semaphore_wait(barrier, nt - 1 + nz - 1 + 2)

    send(xs, xr, x_sem.at[0], x_sem.at[1], other)
    send(kvs.at[c, b], kvs.at[c, b], kv_sem.at[0], kv_sem.at[1], other)
    order = [half]
    for m in range(half - 1, 0, -1):
        order += [m, nz - m]
    order += [0]
    for m in order:
        d = lax.rem(z + m, nz)
        send(w_ref.at[d, o], ws.at[c, d], w_ss.at[d], w_rs.at[d], other)

    fg = [(x, y), (y, x)]

    def at_xy(h, f, g):
        return (f, g) if h == 0 else (g, f)

    def slot(h, f, g):
        x_, y_ = at_xy(h, f, g)
        return mem.at[h, y_ % 2, x_, y_ // 2]

    def place(h, f, g):
        x_, y_ = at_xy(h, f, g)
        return dev(x_, y_, z, c)

    def along_f(h, off):
        f, g = fg[h]
        s = slot(h, f, g)
        send(s, s, ag_ss.at[h, off - 1], ag_rs.at[h, off - 1], place(h, (f + off) % 4, g))

    def from_f(h, off):
        f, g = fg[h]
        arrived(slot(h, (f + 4 - off) % 4, g), ag_ss.at[h, off - 1], ag_rs.at[h, off - 1])

    def along_g(h, i, off):
        f, g = fg[h]
        s = slot(h, (f + i) % 4, g)
        k = 3 + 3 * i + off - 1
        send(s, s, ag_ss.at[h, k], ag_rs.at[h, k], place(h, f, (g + off) % 4))

    def from_g(h, i, off):
        f, g = fg[h]
        k = 3 + 3 * i + off - 1
        arrived(slot(h, (f + i) % 4, (g + 4 - off) % 4), ag_ss.at[h, k], ag_rs.at[h, k])

    arrived(xr, x_sem.at[0], x_sem.at[1])
    for h in range(2):
        for s in range(half):
            mine = own_cols[h * half + s]
            theirs = xr[:, (h * half + s) * 128 : (h * half + s + 1) * 128].astype(F32)
            both = jnp.concatenate(
                [jnp.where(c == 0, mine, theirs), jnp.where(c == 0, theirs, mine)], axis=0
            )
            mem[h, b, x, yh, :, s * 128 : (s + 1) * 128] = both.astype(BF16)
        if h == 0:
            for off in (1, 3, 2):
                along_f(0, off)
            along_g(0, 0, 2)
    along_f(1, 2)
    for off in (1, 3, 2):
        along_g(1, 0, off)
    for off in (1, 3):
        along_f(1, off)
        along_g(0, 0, off)

    def gather_own():
        for off in (1, 3, 2):
            from_f(0, off)
            along_g(0, (4 - off) % 4, 2)
        from_f(1, 2)
        for off in (1, 3, 2):
            along_g(1, 2, off)

    def gather_rest():
        for off in (1, 3):
            from_f(1, off)
        for i in (1, 3, 2):
            for off in (1, 3):
                along_g(0, i, off)
        for i in (1, 3):
            for off in (1, 3, 2):
                along_g(1, i, off)
        send(kvs.at[c, b], kvs.at[c, b], kv_sem.at[2], kv_sem.at[3], dev(x, yh * 2 + (1 - b), z, c))

    def own_gathered(h):
        if h == 0:
            for i in range(4):
                from_g(0, i, 2)
        else:
            for i in (0, 2):
                for off in (1, 3, 2):
                    from_g(1, i, off)

    def rest_gathered(h):
        if h == 0:
            for i in range(4):
                for off in (1, 3):
                    from_g(0, i, off)
        else:
            for i in (1, 3):
                for off in (1, 3, 2):
                    from_g(1, i, off)

    w_load.wait()
    arrived(kvs.at[o, b], kv_sem.at[0], kv_sem.at[1])

    def term(m):
        d = lax.rem(z + m, nz)
        arrived(ws.at[o, d], w_ss.at[d], w_rs.at[d])
        out = lax.dot_general(kvs[0, b], ws[0, d], NT, preferred_element_type=F32)
        out += lax.dot_general(kvs[1, b], ws[1, d], NT, preferred_element_type=F32)
        tm[d] = out * act

    def hop(k, started):
        for j in range(PARTS):
            for d in range(2):
                start = half if (j < PARTS // 2) == (d == 0) else half - 1
                m = start - k
                if m < 1 or (k == 0 and started != (start == half)):
                    continue
                mine = tm[lax.rem(z + (m, nz - m)[d], nz), j * sub : (j + 1) * sub]
                if k == 0:
                    src = first.at[d, j]
                    src[...] = mine.astype(BF16)
                else:
                    src = run.at[d, j, m]
                    arrived(src, z_ss.at[d, j, m], z_rs.at[d, j, m])
                    src[...] = (src[...].astype(F32) + mine).astype(BF16)
                to = dev(x, y, lax.rem(z + (1, nz - 1)[d], nz), c)
                send(src, run.at[d, j, m - 1], z_ss.at[d, j, m - 1], z_rs.at[d, j, m - 1], to)

    def terms(*ms):
        for m in ms:
            term(m)

    def row_dots():
        for h in range(2):
            own_gathered(h)
        for r in range(X):
            acc = jnp.zeros((sub, 128), F32)
            for s in range(nz):
                at = (s % half) * 128
                m = mem[s // half, b, r, :, :, at : at + 128].reshape(sub, 128)
                acc += tm[s, r * sub : (r + 1) * sub] * m.astype(F32)
            qa[r * sub : (r + 1) * sub] = acc
        total = lax.dot_general(
            jnp.ones((8, 128), F32),
            qa[...],
            NT,
            precision=lax.Precision.HIGHEST,
            preferred_element_type=F32,
        )
        hs[...] = total[:1]
        hr[z] = total[:1]
        for i in (8, 7, 9, 6, 10, 5, 11, 4, 12, 3, 13, 2, 14, 1, 15):
            to = lax.rem(z + i, nz)
            send(hs, hr.at[z], h_ss.at[to], h_rs.at[z], (to, t, b))

    def kv_forward():
        got = kvs.at[c, 1 - b]
        arrived(got, kv_sem.at[2], kv_sem.at[3])
        send(got, got, kv_sem.at[4], kv_sem.at[5], other)

    outs = []

    def weight_pass(h, last):
        rep = 1 - b if last else b
        for k in range(cols // 256):
            lhs = mem[h, rep, :, :, :, k * 256 : (k + 1) * 256].reshape(tok, 256)
            part = pl.ds(h * half + 2 * k, 2)
            for side in (1, 0):
                out = lax.dot_general(
                    lhs, kvs[(c, o)[side], rep], TN, preferred_element_type=F32
                )
                out = (out * act).astype(BF16).reshape(2, 128, out.shape[1])
                if last:
                    out = (ow[side, part].astype(F32) + out.astype(F32)).astype(BF16)
                ow[side, part] = out
                n = h * (cols // 256) + k
                if last and side:
                    send(ow.at[1, part], wg_ref.at[part, c], o_sem.at[0, n], o_sem.at[1, n], other)
                elif last:
                    copy = pltpu.make_async_copy(ow.at[0, part], wg_ref.at[part, c], o_sem.at[2, n])
                    copy.start()
                    outs.append(copy)

    def own_weights():
        for h in range(2):
            weight_pass(h, False)

    def row_dot_sums():
        for i in range(1, nz):
            frm = lax.rem(z + i, nz)
            arrived(hr.at[frm], h_ss.at[frm], h_rs.at[frm])
        total = jnp.zeros((1, tok), F32)
        for i in range(nz):
            total += hr[i]
        qs[...] = total
        qr[t] = total
        for i in range(1, nt):
            to = lax.rem(t + i, nt)
            send(qs, qr.at[t], q_ss.at[to], q_rs.at[t], (z, to, b))

    terms(half)
    hop(0, True)
    terms(half - 1, half + 1)
    hop(0, False)
    inner = list(range(half - 2, 0, -1))
    pairs = [(m, nz - m) for m in inner]
    events = {
        0: [lambda: terms(*pairs[0], *pairs[1])],
        1: [gather_own, lambda: terms(*pairs[2], *pairs[3])],
        2: [gather_rest, lambda: terms(*pairs[4], *pairs[5], 0)],
        4: [row_dots],
        5: [own_weights, kv_forward],
        7: [row_dot_sums],
    }
    for k in range(half):
        if k:
            hop(k, True)
        for event in events.get(k, ()):
            event()

    own = lax.rem(z, nz)
    per = nt // PARTS
    for j in range(PARTS):
        total = tm[own, j * sub : (j + 1) * sub]
        for d in range(2):
            arrived(run.at[d, j, 0], z_ss.at[d, j, 0], z_rs.at[d, j, 0])
            total += run[d, j, 0].astype(F32)
        for i in range(per):
            gs[j * per + i] = total[i * rows : (i + 1) * rows].astype(BF16)
    for i in range(1, nt):
        to = lax.rem(t + i, nt)
        send(gs.at[to], gr.at[t], t_ss.at[to], t_rs.at[t], (z, to, b))
    gr[t] = gs[t]

    arrived(kvs.at[o, 1 - b], kv_sem.at[4], kv_sem.at[5])
    for h in range(2):
        rest_gathered(h)
        weight_pass(h, True)

    for i in range(1, nt):
        frm = lax.rem(t + i, nt)
        arrived(gr.at[frm], t_ss.at[frm], t_rs.at[frm])
        arrived(qr.at[frm], q_ss.at[frm], q_rs.at[frm])
    sums = [jnp.zeros((rows, 128), F32), jnp.zeros((rows, 128), F32)]
    row = jnp.zeros((1, tok), F32)
    for i in range(nt):
        sums[i % 2] += gr[i].astype(F32)
        row += qr[i]
    mine = pl.ds(pl.multiple_of(z * 256, 256), 256)
    normed = enc_ref[:, mine] * inv
    scaled = gain_ref[:, mine] * jnp.concatenate(sums, axis=1)
    token = lax.broadcasted_iota(jnp.int32, (rows, tok), 0) + t * rows
    here = token == lax.broadcasted_iota(jnp.int32, (rows, tok), 1)
    row_dot = jnp.sum(jnp.where(here, row, 0.0), axis=1, keepdims=True) * (1.0 / width)
    eg_ref[...] = (inv * (scaled - normed * row_dot)).astype(BF16)

    for n in range(nz // 2):
        part = pl.ds(2 * n, 2)
        arrived(wg_ref.at[part, o], o_sem.at[0, n], o_sem.at[1, n])
    for copy in outs:
        copy.wait()
    for copy in sent:
        copy.wait_send()


def solution(mesh):
    nz, nt = mesh.shape["section"], mesh.shape["tensor"]

    def per_device(enc_out, gain, weights, kv_grad):
        _, rows, width = enc_out.shape
        tok, hd = kv_grad.shape[2:]
        half = nz // 2
        dma = pltpu.SemaphoreType.DMA
        wg, eg = pl.pallas_call(
            functools.partial(kernel, nz),
            out_shape=(
                jax.ShapeDtypeStruct((nz, 2, 128, hd), BF16),
                jax.ShapeDtypeStruct((rows, 256), BF16),
            ),
            in_specs=[pl.BlockSpec(memory_space=pltpu.HBM)] * 4,
            out_specs=(
                pl.BlockSpec(memory_space=pl.ANY),
                pl.BlockSpec(memory_space=pltpu.VMEM),
            ),
            scratch_shapes=[
                pltpu.VMEM((rows, width), F32),
                pltpu.VMEM((1, width), F32),
                pltpu.VMEM((rows, width // 2), BF16),
                pltpu.VMEM((rows, width // 2), BF16),
                pltpu.VMEM((2, 2, X, 2, 2 * rows, half * 128), BF16),
                pltpu.VMEM((2, 2, tok, hd), BF16),
                pltpu.VMEM((2, nz, 128, hd), BF16),
                pltpu.VMEM((nz, tok, 128), F32),
                pltpu.VMEM((2, PARTS, tok // PARTS, 128), BF16),
                pltpu.VMEM((2, PARTS, half, tok // PARTS, 128), BF16),
                pltpu.VMEM((nt, rows, 128), BF16),
                pltpu.VMEM((nt, rows, 128), BF16),
                pltpu.VMEM((tok, 128), F32),
                pltpu.VMEM((1, tok), F32),
                pltpu.VMEM((nz, 1, tok), F32),
                pltpu.VMEM((1, tok), F32),
                pltpu.VMEM((nt, 1, tok), F32),
                pltpu.VMEM((2, nz, 128, hd), BF16),
                dma((4,)),
                dma((2,)),
                dma((6,)),
                dma((nz,)),
                dma((nz,)),
                dma((2, 15)),
                dma((2, 15)),
                dma((2, PARTS, half)),
                dma((2, PARTS, half)),
                dma((nt,)),
                dma((nt,)),
                dma((nt,)),
                dma((nt,)),
                dma((nz,)),
                dma((nz,)),
                dma((3, nz // 2)),
            ],
            compiler_params=pltpu.CompilerParams(
                collective_id=0, has_side_effects=True, vmem_limit_bytes=32 * 1024 * 1024
            ),
            cost_estimate=pl.CostEstimate(
                flops=6 * tok * width * hd, bytes_accessed=8 * width * hd, transcendentals=0
            ),
        )(
            enc_out[0],
            gain.reshape(1, width),
            weights.reshape(nz, 2, 128, hd),
            kv_grad[0, 0],
        )
        return wg.reshape(1, width, hd), eg[None]

    return jax.shard_map(
        per_device,
        mesh=mesh,
        in_specs=(
            P("dp", "tensor", None),
            P(),
            P("section", None, "tensor"),
            P("section", "dp", None, "tensor"),
        ),
        out_specs=(P("section", None, "tensor"), P("dp", "tensor", "section")),
        check_vma=False,
    )
```

time: 76.1 us -> 69 us (0.907)
  Pallas kernels: 69.1 us -> 62 us
    pallas_call x1, Pallas kernels: 69.1 us -> 62 us  [per_device(): pl.pallas_call(functools.partial(kernel, nz), out_shape=(jax.ShapeDtypeSt...]
where the time goes in v2:
time: 69 us; the launch traced here: 68.8 us
  Pallas kernels  62 us (90%)
  local copies, waits for them, and re-layouts  6.14 us (9%)
    pallas_call x1, Pallas kernels, per_device(): pl.pallas_call(functools.partial(kernel, nz), out_shape=(jax.ShapeDtypeSt...  62 us
    unnamed x10, local copies, waits for them, and re-layouts  6.14 us

profile of v2, /device:TPU:1, one launch (start us, length us, event | category | flops | bytes accessed | tf_op | source)
XLA Modules:
  0.0 68.8 jit_solution(15645118338174680729)
XLA Ops:
  0.6 0.0 copy-start
  0.6 1.6 %copy-done = bf16[1,4096,256]{2,1,0:T(8,128)(2,1)S(1)} copy-done((bf16[1,4096,256]{2,1,0:T(8,128)(2,1)S(1)}, bf16[1,4096,256]{2,1,0:T(8,128)(2,1)}, u32[]{:S(2)}) %copy-start) | copy-done | bytes 2097176
  2.2 0.0 copy-start.1
  2.2 1.0 %copy-done.1 = f32[1,24,4096]{2,1,0:T(8,128)S(1)} copy-done((f32[1,24,4096]{2,1,0:T(8,128)S(1)}, f32[1,24,4096]{2,1,0:T(8,128)}, u32[]{:S(2)}) %copy-start.1) | copy-done | bytes 393240
  3.2 0.0 copy-start.2
  3.2 0.9 %copy-done.2 = bf16[1,1,384,256]{3,2,1,0:T(8,128)(2,1)S(1)} copy-done((bf16[1,1,384,256]{3,2,1,0:T(8,128)(2,1)S(1)}, bf16[1,1,384,256]{3,2,1,0:T(8,128)(2,1)}, u32[]{:S(2)}) %copy-start.2) | copy-done | bytes 196632
  4.1 0.0 copy-start.3
  4.1 0.7 %copy-done.3 = f32[4096]{0:T(1024)S(1)} copy-done((f32[4096]{0:T(1024)S(1)}, f32[4096]{0:T(1024)}, u32[]{:S(2)}) %copy-start.3) | copy-done | bytes 16408
  4.9 62.0 %shard_map.59 = (bf16[16,2,128,256]{3,2,1,0:T(8,128)(2,1)S(1)}, bf16[24,256]{1,0:T(8,128)(2,1)S(1)}) custom-call(f32[24,4096]{1,0:T(8,128)S(1)} %bitcast.9, f32[1,4096]{1,0:T(1,128)S(1)} %bitcast.11, bf16[16,2,128,256]{3,2,1,0:T(8,128)(2,1)S(1)} %bitcast.8, bf16[384,256]{1,0:T(8,128)(2,1)S(1)} %bitcast.10), custom_call_target="tpu_custom_call" | custom-call | flops 2415919104 | bytes 8388608 | tf_op jit(solution)/shard_map/pallas_call | solution.py:405
  66.9 1.3 %copy.8 = bf16[1,4096,256]{2,1,0:T(8,128)(2,1)} copy(bf16[1,4096,256]{2,1,0:T(8,128)(2,1)S(1)} %bitcast.6) | data formatting | bytes 4194304
  68.2 0.6 copy.9
Async XLA Ops:
  0.6 1.6 %copy-start = (bf16[1,4096,256]{2,1,0:T(8,128)(2,1)S(1)}, bf16[1,4096,256]{2,1,0:T(8,128)(2,1)}, u32[]{:S(2)}) copy-start(bf16[1,4096,256]{2,1,0:T(8,128)(2,1)} %param.6) | copy-start | bytes 6291460
  2.2 1.0 %copy-start.1 = (f32[1,24,4096]{2,1,0:T(8,128)S(1)}, f32[1,24,4096]{2,1,0:T(8,128)}, u32[]{:S(2)}) copy-start(f32[1,24,4096]{2,1,0:T(8,128)} %param.4) | copy-start | bytes 1179652
  3.2 0.9 %copy-start.2 = (bf16[1,1,384,256]{3,2,1,0:T(8,128)(2,1)S(1)}, bf16[1,1,384,256]{3,2,1,0:T(8,128)(2,1)}, u32[]{:S(2)}) copy-start(bf16[1,1,384,256]{3,2,1,0:T(8,128)(2,1)} %param.7) | copy-start | bytes 589828
  4.1 0.7 %copy-start.3 = (f32[4096]{0:T(1024)S(1)}, f32[4096]{0:T(1024)}, u32[]{:S(2)}) copy-start(f32[4096]{0:T(1024)} %param.5) | copy-start | bytes 49156

commit v3 on v2

--- a/solution.py
+++ b/solution.py
@@ -83,12 +83,19 @@
         )
 
     other = dev(x, y, z, o)
-    sent = []
-
-    def send(src, dst, ss, rs, to):
+    sent, gathers, marks = [], [], [0]
+
+    def send(src, dst, ss, rs, to, copies=sent):
         copy = remote(src, dst, ss, rs, to)
         copy.start()
-        sent.append(copy)
+        copies.append(copy)
+
+    waited = [0]
+
+    def flush(n):
+        for copy in sent[waited[0] : n]:
+            copy.wait_send()
+        waited[0] = n
 
     def arrived(dst, ss, rs):
         remote(dst, dst, ss, rs, other).wait_recv()
@@ -130,13 +137,19 @@
 
     send(xs, xr, x_sem.at[0], x_sem.at[1], other)
     send(kvs.at[c, b], kvs.at[c, b], kv_sem.at[0], kv_sem.at[1], other)
-    order = [half]
-    for m in range(half - 1, 0, -1):
-        order += [m, nz - m]
+    npair = nz // 2
+    order = [npair // 2]
+    for r in range(npair // 2 - 1, 0, -1):
+        order += [r, npair - r]
     order += [0]
-    for m in order:
-        d = lax.rem(z + m, nz)
-        send(w_ref.at[d, o], ws.at[c, d], w_ss.at[d], w_rs.at[d], other)
+
+    def pair(r):
+        return lax.rem(z // 2 + r, npair)
+
+    for r in order:
+        p = pair(r)
+        ds = pl.ds(2 * p, 2)
+        send(w_ref.at[ds, o], ws.at[c, ds], w_ss.at[p], w_rs.at[p], other)
 
     fg = [(x, y), (y, x)]
 
@@ -154,7 +167,8 @@
     def along_f(h, off):
         f, g = fg[h]
         s = slot(h, f, g)
-        send(s, s, ag_ss.at[h, off - 1], ag_rs.at[h, off - 1], place(h, (f + off) % 4, g))
+        to = place(h, (f + off) % 4, g)
+        send(s, s, ag_ss.at[h, off - 1], ag_rs.at[h, off - 1], to, gathers)
 
     def from_f(h, off):
         f, g = fg[h]
@@ -164,7 +178,7 @@
         f, g = fg[h]
         s = slot(h, (f + i) % 4, g)
         k = 3 + 3 * i + off - 1
-        send(s, s, ag_ss.at[h, k], ag_rs.at[h, k], place(h, f, (g + off) % 4))
+        send(s, s, ag_ss.at[h, k], ag_rs.at[h, k], place(h, f, (g + off) % 4), gathers)
 
     def from_g(h, i, off):
         f, g = fg[h]
@@ -183,13 +197,15 @@
         if h == 0:
             for off in (1, 3, 2):
                 along_f(0, off)
-            along_g(0, 0, 2)
     along_f(1, 2)
-    for off in (1, 3, 2):
-        along_g(1, 0, off)
-    for off in (1, 3):
-        along_f(1, off)
-        along_g(0, 0, off)
+
+    def gather_start():
+        along_g(0, 0, 2)
+        for off in (1, 3, 2):
+            along_g(1, 0, off)
+        for off in (1, 3):
+            along_f(1, off)
+            along_g(0, 0, off)
 
     def gather_own():
         for off in (1, 3, 2):
@@ -208,7 +224,8 @@
         for i in (1, 3):
             for off in (1, 3, 2):
                 along_g(1, i, off)
-        send(kvs.at[c, b], kvs.at[c, b], kv_sem.at[2], kv_sem.at[3], dev(x, yh * 2 + (1 - b), z, c))
+        mine = kvs.at[c, b]
+        send(mine, mine, kv_sem.at[2], kv_sem.at[3], dev(x, yh * 2 + (1 - b), z, c), gathers)
 
     def own_gathered(h):
         if h == 0:
@@ -232,12 +249,17 @@
     w_load.wait()
     arrived(kvs.at[o, b], kv_sem.at[0], kv_sem.at[1])
 
-    def term(m):
-        d = lax.rem(z + m, nz)
-        arrived(ws.at[o, d], w_ss.at[d], w_rs.at[d])
-        out = lax.dot_general(kvs[0, b], ws[0, d], NT, preferred_element_type=F32)
-        out += lax.dot_general(kvs[1, b], ws[1, d], NT, preferred_element_type=F32)
-        tm[d] = out * act
+    def term(r):
+        p = pair(r)
+        ds = pl.ds(2 * p, 2)
+        arrived(ws.at[o, ds], w_ss.at[p], w_rs.at[p])
+        out = jnp.zeros((tok, 256), F32)
+        for core in range(2):
+            rhs = ws[core, ds].reshape(256, ws.shape[3])
+            out += lax.dot_general(kvs[core, b], rhs, NT, preferred_element_type=F32)
+        out *= act
+        tm[2 * p] = out[:, :128]
+        tm[2 * p + 1] = out[:, 128:]
 
     def hop(k, started):
         for j in range(PARTS):
@@ -257,9 +279,9 @@
                 to = dev(x, y, lax.rem(z + (1, nz - 1)[d], nz), c)
                 send(src, run.at[d, j, m - 1], z_ss.at[d, j, m - 1], z_rs.at[d, j, m - 1], to)
 
-    def terms(*ms):
-        for m in ms:
-            term(m)
+    def terms(*rs):
+        for r in rs:
+            term(r)
 
     def row_dots():
         for h in range(2):
@@ -329,18 +351,17 @@
             to = lax.rem(t + i, nt)
             send(qs, qr.at[t], q_ss.at[to], q_rs.at[t], (z, to, b))
 
-    terms(half)
+    term(order[0])
     hop(0, True)
-    terms(half - 1, half + 1)
+    gather_start()
+    terms(*order[1:3])
     hop(0, False)
-    inner = list(range(half - 2, 0, -1))
-    pairs = [(m, nz - m) for m in inner]
     events = {
-        0: [lambda: terms(*pairs[0], *pairs[1])],
-        1: [gather_own, lambda: terms(*pairs[2], *pairs[3])],
-        2: [gather_rest, lambda: terms(*pairs[4], *pairs[5], 0)],
-        4: [row_dots],
-        5: [own_weights, kv_forward],
+        0: [lambda: terms(*order[3:5])],
+        1: [gather_own, lambda: terms(*order[5:7])],
+        2: [gather_rest, lambda: terms(order[7])],
+        5: [row_dots],
+        6: [own_weights, kv_forward],
         7: [row_dot_sums],
     }
     for k in range(half):
@@ -348,6 +369,9 @@
             hop(k, True)
         for event in events.get(k, ()):
             event()
+        if k >= 2:
+            flush(marks[k - 1])
+        marks.append(len(sent))
 
     own = lax.rem(z, nz)
     per = nt // PARTS
@@ -358,6 +382,7 @@
             total += run[d, j, 0].astype(F32)
         for i in range(per):
             gs[j * per + i] = total[i * rows : (i + 1) * rows].astype(BF16)
+    before_last = len(sent)
     for i in range(1, nt):
         to = lax.rem(t + i, nt)
         send(gs.at[to], gr.at[t], t_ss.at[to], t_rs.at[t], (z, to, b))
@@ -367,6 +392,10 @@
     for h in range(2):
         rest_gathered(h)
         weight_pass(h, True)
+
+    for copy in gathers:
+        copy.wait_send()
+    flush(before_last)
 
     for i in range(1, nt):
         frm = lax.rem(t + i, nt)
@@ -390,8 +419,7 @@
         arrived(wg_ref.at[part, o], o_sem.at[0, n], o_sem.at[1, n])
     for copy in outs:
         copy.wait()
-    for copy in sent:
-        copy.wait_send()
+    flush(len(sent))
 
 
 def solution(mesh):
@@ -435,8 +463,8 @@
                 dma((4,)),
                 dma((2,)),
                 dma((6,)),
-                dma((nz,)),
-                dma((nz,)),
+                dma((nz // 2,)),
+                dma((nz // 2,)),
                 dma((2, 15)),
                 dma((2, 15)),
                 dma((2, PARTS, half)),
@@ -456,10 +484,15 @@
                 flops=6 * tok * width * hd, bytes_accessed=8 * width * hd, transcendentals=0
             ),
         )(
-            enc_out[0],
-            gain.reshape(1, width),
-            weights.reshape(nz, 2, 128, hd),
-            kv_grad[0, 0],
+            *(
+                pltpu.with_memory_space_constraint(a, pltpu.HBM)
+                for a in (
+                    enc_out[0],
+                    gain.reshape(1, width),
+                    weights.reshape(nz, 2, 128, hd),
+                    kv_grad[0, 0],
+                )
+            )
         )
         return wg.reshape(1, width, hd), eg[None]
 

time: 69 us -> 60.6 us (0.88)
  local copies, waits for them, and re-layouts: 6.14 us -> 1.92 us
  Pallas kernels: 62 us -> 57.9 us
    unnamed x10 -> x2, local copies, waits for them, and re-layouts: 6.14 us -> 1.92 us
    pallas_call x1, Pallas kernels: 62 us -> 57.9 us  [per_device(): pl.pallas_call(functools.partial(kernel, nz), out_shape=(jax.ShapeDtypeSt...]
where the time goes in v3:
time: 60.6 us; the launch traced here: 60.5 us
  Pallas kernels  57.9 us (96%)
  local copies, waits for them, and re-layouts  1.92 us (3%)
  between operations  0.64 us (1%)
    pallas_call x1, Pallas kernels, per_device(): pl.pallas_call(functools.partial(kernel, nz), out_shape=(jax.ShapeDtypeSt...  57.9 us
    unnamed x2, local copies, waits for them, and re-layouts  1.92 us

profile of v3, /device:TPU:1, one launch (start us, length us, event | category | flops | bytes accessed | tf_op | source)
XLA Modules:
  0.0 60.5 jit_solution(18260392477168084709)
XLA Ops:
  0.6 57.9 %shard_map.59 = (bf16[16,2,128,256]{3,2,1,0:T(8,128)(2,1)S(1)}, bf16[24,256]{1,0:T(8,128)(2,1)S(1)}) custom-call(f32[24,4096]{1,0:T(8,128)} %bitcast.9, f32[1,4096]{1,0:T(1,128)} %bitcast.11, bf16[16,2,128,256]{3,2,1,0:T(8,128)(2,1)} %bitcast.8, bf16[384,256]{1,0:T(8,128)(2,1)} %bitcast.10), custom_call_target="tpu_custom_call" | custom-call | flops 2415919104 | bytes 8388608 | tf_op jit(solution)/shard_map/pallas_call | solution.py:433
  58.6 1.3 %copy.8 = bf16[1,4096,256]{2,1,0:T(8,128)(2,1)} copy(bf16[1,4096,256]{2,1,0:T(8,128)(2,1)S(1)} %bitcast.6) | data formatting | bytes 4194304
  59.9 0.6 copy.9

commit v4 on v3

--- a/solution.py
+++ b/solution.py
@@ -56,6 +56,7 @@
     h_ss,
     h_rs,
     o_sem,
+    hello,
 ):
     z, t, b = lax.axis_index("section"), lax.axis_index("tensor"), lax.axis_index("dp")
     x, yh, c = t // 4, (t // 2) % 2, t % 2
@@ -100,18 +101,6 @@
     def arrived(dst, ss, rs):
         remote(dst, dst, ss, rs, other).wait_recv()
 
-    barrier = pltpu.get_barrier_semaphore()
-
-    def greet(to):
-        pl.semaphore_signal(barrier, inc=1, device_id=to, device_id_type=pl.DeviceIdType.MESH)
-
-    for i in (8, 7, 9, 6, 10, 5, 11, 4, 12, 3, 13, 2, 14, 1, 15):
-        greet((lax.rem(z + i, nz), t, b))
-    for i in range(1, nt):
-        greet((z, lax.rem(t + i, nt), b))
-    greet(dev(x, (y + 1) % Y, z, c))
-    greet(dev(x, (y + 3) % Y, z, c))
-
     enc_load = pltpu.make_async_copy(enc_hbm, enc_ref, loc_sem.at[2])
     enc_load.start()
     gain_load = pltpu.make_async_copy(gain_hbm, gain_ref, loc_sem.at[3])
@@ -120,6 +109,20 @@
     kv_load.start()
     w_load = pltpu.make_async_copy(w_ref.at[:, c], ws.at[c], loc_sem.at[1])
     w_load.start()
+
+    barrier = pltpu.get_barrier_semaphore()
+
+    def greet(to):
+        pl.semaphore_signal(barrier, inc=1, device_id=to, device_id_type=pl.DeviceIdType.MESH)
+
+    greet(other)
+    far = half // 2
+    for i in (1, nz - 1, far, nz - far):
+        greet((lax.rem(z + i, nz), t, b))
+    for i in range(1, X):
+        greet(dev((x + i) % X, y, z, c))
+    for i in range(1, Y):
+        greet(dev(x, (y + i) % Y, z, c))
 
     enc_load.wait()
     gain_load.wait()
@@ -133,7 +136,7 @@
         xs[:, s * 128 : (s + 1) * 128] = jnp.where(c == 0, hi, lo).astype(BF16)
     kv_load.wait()
 
-    pl.semaphore_wait(barrier, nt - 1 + nz - 1 + 2)
+    pl.semaphore_wait(barrier, 1 + 4 + X - 1 + Y - 1)
 
     send(xs, xr, x_sem.at[0], x_sem.at[1], other)
     send(kvs.at[c, b], kvs.at[c, b], kv_sem.at[0], kv_sem.at[1], other)
@@ -283,16 +286,22 @@
         for r in rs:
             term(r)
 
+    def say_hello():
+        for i in (far, nz - far):
+            to = (lax.rem(z + i, nz), t, b)
+            pl.semaphore_signal(hello, inc=1, device_id=to, device_id_type=pl.DeviceIdType.MESH)
+
     def row_dots():
         for h in range(2):
             own_gathered(h)
+        blk = tok // X
         for r in range(X):
-            acc = jnp.zeros((sub, 128), F32)
+            acc = jnp.zeros((blk, 128), F32)
             for s in range(nz):
                 at = (s % half) * 128
-                m = mem[s // half, b, r, :, :, at : at + 128].reshape(sub, 128)
-                acc += tm[s, r * sub : (r + 1) * sub] * m.astype(F32)
-            qa[r * sub : (r + 1) * sub] = acc
+                m = mem[s // half, b, r, :, :, at : at + 128].reshape(blk, 128)
+                acc += tm[s, r * blk : (r + 1) * blk] * m.astype(F32)
+            qa[r * blk : (r + 1) * blk] = acc
         total = lax.dot_general(
             jnp.ones((8, 128), F32),
             qa[...],
@@ -302,6 +311,7 @@
         )
         hs[...] = total[:1]
         hr[z] = total[:1]
+        pl.semaphore_wait(hello, 2)
         for i in (8, 7, 9, 6, 10, 5, 11, 4, 12, 3, 13, 2, 14, 1, 15):
             to = lax.rem(z + i, nz)
             send(hs, hr.at[z], h_ss.at[to], h_rs.at[z], (to, t, b))
@@ -360,6 +370,7 @@
         0: [lambda: terms(*order[3:5])],
         1: [gather_own, lambda: terms(*order[5:7])],
         2: [gather_rest, lambda: terms(order[7])],
+        4: [say_hello],
         5: [row_dots],
         6: [own_weights, kv_forward],
         7: [row_dot_sums],
@@ -373,21 +384,22 @@
             flush(marks[k - 1])
         marks.append(len(sent))
 
-    own = lax.rem(z, nz)
     per = nt // PARTS
+
+    def piece(i):
+        return remote(gs.at[i], gr.at[t], t_ss.at[i], t_rs.at[t], (z, i, b))
+
     for j in range(PARTS):
-        total = tm[own, j * sub : (j + 1) * sub]
+        total = tm[z, j * sub : (j + 1) * sub]
         for d in range(2):
             arrived(run.at[d, j, 0], z_ss.at[d, j, 0], z_rs.at[d, j, 0])
             total += run[d, j, 0].astype(F32)
-        for i in range(per):
-            gs[j * per + i] = total[i * rows : (i + 1) * rows].astype(BF16)
-    before_last = len(sent)
-    for i in range(1, nt):
-        to = lax.rem(t + i, nt)
-        send(gs.at[to], gr.at[t], t_ss.at[to], t_rs.at[t], (z, to, b))
+        for i in range(j * per, (j + 1) * per):
+            r = (i - j * per) * rows
+            gs[i] = total[r : r + rows].astype(BF16)
+        for i in range(j * per, (j + 1) * per):
+            pl.when(i != t)(piece(i).start)
     gr[t] = gs[t]
-
     arrived(kvs.at[o, 1 - b], kv_sem.at[4], kv_sem.at[5])
     for h in range(2):
         rest_gathered(h)
@@ -395,23 +407,26 @@
 
     for copy in gathers:
         copy.wait_send()
-    flush(before_last)
-
+    flush(len(sent) - nz // 2)
+
+    for i in range(1, nt):
+        frm = lax.rem(t + i, nt)
+        arrived(qr.at[frm], q_ss.at[frm], q_rs.at[frm])
+    row = jnp.zeros((1, tok), F32)
+    for i in range(nt):
+        row += qr[i]
+    mine = pl.ds(pl.multiple_of(z * 256, 256), 256)
+    normed = enc_ref[:, mine] * inv
+    token = lax.broadcasted_iota(jnp.int32, (rows, tok), 0) + t * rows
+    here = token == lax.broadcasted_iota(jnp.int32, (rows, tok), 1)
+    row_dot = jnp.sum(jnp.where(here, row, 0.0), axis=1, keepdims=True) * (1.0 / width)
     for i in range(1, nt):
         frm = lax.rem(t + i, nt)
         arrived(gr.at[frm], t_ss.at[frm], t_rs.at[frm])
-        arrived(qr.at[frm], q_ss.at[frm], q_rs.at[frm])
     sums = [jnp.zeros((rows, 128), F32), jnp.zeros((rows, 128), F32)]
-    row = jnp.zeros((1, tok), F32)
     for i in range(nt):
         sums[i % 2] += gr[i].astype(F32)
-        row += qr[i]
-    mine = pl.ds(pl.multiple_of(z * 256, 256), 256)
-    normed = enc_ref[:, mine] * inv
     scaled = gain_ref[:, mine] * jnp.concatenate(sums, axis=1)
-    token = lax.broadcasted_iota(jnp.int32, (rows, tok), 0) + t * rows
-    here = token == lax.broadcasted_iota(jnp.int32, (rows, tok), 1)
-    row_dot = jnp.sum(jnp.where(here, row, 0.0), axis=1, keepdims=True) * (1.0 / width)
     eg_ref[...] = (inv * (scaled - normed * row_dot)).astype(BF16)
 
     for n in range(nz // 2):
@@ -420,6 +435,8 @@
     for copy in outs:
         copy.wait()
     flush(len(sent))
+    for i in range(nt):
+        pl.when(i != t)(piece(i).wait_send)
 
 
 def solution(mesh):
@@ -476,6 +493,7 @@
                 dma((nz,)),
                 dma((nz,)),
                 dma((3, nz // 2)),
+                pltpu.SemaphoreType.REGULAR,
             ],
             compiler_params=pltpu.CompilerParams(
                 collective_id=0, has_side_effects=True, vmem_limit_bytes=32 * 1024 * 1024

time: 60.6 us -> 58.3 us (0.962)
  Pallas kernels: 57.9 us -> 55.6 us
    pallas_call x1, Pallas kernels: 57.9 us -> 55.6 us  [per_device(): pl.pallas_call(functools.partial(kernel, nz), out_shape=(jax.ShapeDtypeSt...]
where the time goes in v4:
time: 58.3 us; the launch traced here: 58.1 us
  Pallas kernels  55.6 us (95%)
  local copies, waits for them, and re-layouts  1.92 us (3%)
  between operations  0.64 us (1%)
    pallas_call x1, Pallas kernels, per_device(): pl.pallas_call(functools.partial(kernel, nz), out_shape=(jax.ShapeDtypeSt...  55.6 us
    unnamed x2, local copies, waits for them, and re-layouts  1.92 us

profile of v4, /device:TPU:1, one launch (start us, length us, event | category | flops | bytes accessed | tf_op | source)
XLA Modules:
  0.0 58.1 jit_solution(16816178437926848767)
XLA Ops:
  0.6 55.6 %shard_map.59 = (bf16[16,2,128,256]{3,2,1,0:T(8,128)(2,1)S(1)}, bf16[24,256]{1,0:T(8,128)(2,1)S(1)}) custom-call(f32[24,4096]{1,0:T(8,128)} %bitcast.9, f32[1,4096]{1,0:T(1,128)} %bitcast.11, bf16[16,2,128,256]{3,2,1,0:T(8,128)(2,1)} %bitcast.8, bf16[384,256]{1,0:T(8,128)(2,1)} %bitcast.10), custom_call_target="tpu_custom_call" | custom-call | flops 2415919104 | bytes 8388608 | tf_op jit(solution)/shard_map/pallas_call | solution.py:450
  56.2 1.3 %copy.8 = bf16[1,4096,256]{2,1,0:T(8,128)(2,1)} copy(bf16[1,4096,256]{2,1,0:T(8,128)(2,1)S(1)} %bitcast.6) | data formatting | bytes 4194304
  57.5 0.6 %copy.9 = bf16[1,24,256]{2,1,0:T(8,128)(2,1)} copy(bf16[1,24,256]{2,1,0:T(8,128)(2,1)S(1)} %bitcast.7) | data formatting | bytes 24576

commit v5 on v4

--- a/solution.py
+++ b/solution.py
@@ -117,7 +117,7 @@
 
     greet(other)
     far = half // 2
-    for i in (1, nz - 1, far, nz - far):
+    for i in (1, nz - 1):
         greet((lax.rem(z + i, nz), t, b))
     for i in range(1, X):
         greet(dev((x + i) % X, y, z, c))
@@ -136,7 +136,7 @@
         xs[:, s * 128 : (s + 1) * 128] = jnp.where(c == 0, hi, lo).astype(BF16)
     kv_load.wait()
 
-    pl.semaphore_wait(barrier, 1 + 4 + X - 1 + Y - 1)
+    pl.semaphore_wait(barrier, 1 + 2 + X - 1 + Y - 1)
 
     send(xs, xr, x_sem.at[0], x_sem.at[1], other)
     send(kvs.at[c, b], kvs.at[c, b], kv_sem.at[0], kv_sem.at[1], other)

time: 58.3 us -> 57.7 us (0.990)
  Pallas kernels: 55.6 us -> 55 us
where the time goes in v5:
time: 57.7 us; the launch traced here: 57.5 us
  Pallas kernels  55 us (95%)
  local copies, waits for them, and re-layouts  1.92 us (3%)
  between operations  0.64 us (1%)
    pallas_call x1, Pallas kernels, per_device(): pl.pallas_call(functools.partial(kernel, nz), out_shape=(jax.ShapeDtypeSt...  55 us
    unnamed x2, local copies, waits for them, and re-layouts  1.92 us

profile of v5, /device:TPU:1, one launch (start us, length us, event | category | flops | bytes accessed | tf_op | source)
XLA Modules:
  0.0 57.5 jit_solution(7121457367362963877)
XLA Ops:
  0.6 55.0 %shard_map.59 = (bf16[16,2,128,256]{3,2,1,0:T(8,128)(2,1)S(1)}, bf16[24,256]{1,0:T(8,128)(2,1)S(1)}) custom-call(f32[24,4096]{1,0:T(8,128)} %bitcast.9, f32[1,4096]{1,0:T(1,128)} %bitcast.11, bf16[16,2,128,256]{3,2,1,0:T(8,128)(2,1)} %bitcast.8, bf16[384,256]{1,0:T(8,128)(2,1)} %bitcast.10), custom_call_target="tpu_custom_call" | custom-call | flops 2415919104 | bytes 8388608 | tf_op jit(solution)/shard_map/pallas_call | solution.py:450
  55.6 1.3 %copy.8 = bf16[1,4096,256]{2,1,0:T(8,128)(2,1)} copy(bf16[1,4096,256]{2,1,0:T(8,128)(2,1)S(1)} %bitcast.6) | data formatting | bytes 4194304
  56.9 0.6 %copy.9 = bf16[1,24,256]{2,1,0:T(8,128)(2,1)} copy(bf16[1,24,256]{2,1,0:T(8,128)(2,1)S(1)} %bitcast.7) | data formatting | bytes 24576

commit v6 on v5

--- a/solution.py
+++ b/solution.py
@@ -380,7 +380,7 @@
             hop(k, True)
         for event in events.get(k, ()):
             event()
-        if k >= 2:
+        if 2 <= k < half - 1:
             flush(marks[k - 1])
         marks.append(len(sent))
 

time: 57.7 us -> 57.7 us (level)
  no operation moved by 1% of the time
where the time goes in v6:
time: 57.7 us; the launch traced here: 57.5 us
  Pallas kernels  55 us (95%)
  local copies, waits for them, and re-layouts  1.92 us (3%)
  between operations  0.64 us (1%)
    pallas_call x1, Pallas kernels, per_device(): pl.pallas_call(functools.partial(kernel, nz), out_shape=(jax.ShapeDtypeSt...  55 us
    unnamed x2, local copies, waits for them, and re-layouts  1.92 us

profile of v6, /device:TPU:1, one launch (start us, length us, event | category | flops | bytes accessed | tf_op | source)
XLA Modules:
  0.0 57.5 jit_solution(11222095809286726909)
XLA Ops:
  0.6 55.0 %shard_map.59 = (bf16[16,2,128,256]{3,2,1,0:T(8,128)(2,1)S(1)}, bf16[24,256]{1,0:T(8,128)(2,1)S(1)}) custom-call(f32[24,4096]{1,0:T(8,128)} %bitcast.9, f32[1,4096]{1,0:T(1,128)} %bitcast.11, bf16[16,2,128,256]{3,2,1,0:T(8,128)(2,1)} %bitcast.8, bf16[384,256]{1,0:T(8,128)(2,1)} %bitcast.10), custom_call_target="tpu_custom_call" | custom-call | flops 2415919104 | bytes 8388608 | tf_op jit(solution)/shard_map/pallas_call | solution.py:450
  55.6 1.3 %copy.8 = bf16[1,4096,256]{2,1,0:T(8,128)(2,1)} copy(bf16[1,4096,256]{2,1,0:T(8,128)(2,1)S(1)} %bitcast.6) | data formatting | bytes 4194304
  56.9 0.6 %copy.9 = bf16[1,24,256]{2,1,0:T(8,128)(2,1)} copy(bf16[1,24,256]{2,1,0:T(8,128)(2,1)S(1)} %bitcast.7) | data formatting | bytes 24576
